TPU v7x, 32 devices: a whole 2x2x4 slice. The times are simulated.
32 devices in a mesh: groups: 2 (over y), tp: 4 (over z), sub: 4 (over x, core).
Axes of the slice: x: 2, y: 2, z: 4, core: 2. Of those that a mesh axis runs over, the one named last changes fastest.
Arguments:
- queries: bfloat16 [8, 64, 16384], P(('groups', 'sub'), None, 'tp'), parts along dimension 0, may hold values from -128 to 128
- block_kv: bfloat16 [8, 64, 2, 512], P(('groups', 'sub'), None, None, 'tp'), parts along dimension 0, may hold values from -64 to 64
- cache_kv: bfloat16 [8, 2, 4, 1024, 128], P(('groups', 'sub'), None, 'tp'), parts along dimension 0, may hold values from -64 to 64
- prefix_len: int32 [8], P(('groups', 'sub')), parts along dimension 0, may hold values from 128 to 1024, as said below
- residual: bfloat16 [512, 16384], P(('groups', 'tp'), 'sub'), parts along dimension 0, may hold values from -3 to 3
- out_weight: bfloat16 [16384, 16384], P('tp', 'sub'), may hold values from -0.375 to 0.375
Outputs:
- mixed: bfloat16 [512, 16384], P('groups', 'sub'), parts along dimension 0
There are 2 independent parts, one for each index of `groups`. A program takes and returns all parts, laid end to end along the dimension named above; an argument that names none is the same for every part. Nothing has to cross between parts.
Inputs may be any that keep to these rules, and one draw needn't show every extreme that they name: `prefix_len`: cache slots below a request's length hold its prefix; some request has exactly 1024.
All inputs are finite; a program needn't handle non-finite values.
Results may differ from a plain program's by a relative error of at most 0.0062.
Values may be sent and summed in bfloat16 or wider, within the bound.
A program may use at most 128 MiB of HBM per device.

v0:
```python
import jax
import jax.numpy as jnp
from jax import lax
from jax.sharding import PartitionSpec as P

HD = 128


def attend_local(queries, block_kv, cache_kv, prefix_len):
    req_count, steps, width = queries.shape
    group = width // HD
    capacity = cache_kv.shape[3]
    heads_q = queries.reshape(req_count, steps, group, HD)
    block_keys = block_kv[:, :, 0, :]
    block_vals = block_kv[:, :, 1, :]
    cache_keys = cache_kv[:, 0, 0]
    cache_vals = cache_kv[:, 1, 0]
    scale = HD ** (-0.5)
    cached = (
        jnp.einsum("rcgd,rpd->rgcp", heads_q, cache_keys, preferred_element_type=jnp.float32)
        * scale
    )
    valid = jnp.arange(capacity)[None, :] < prefix_len[:, None]
    cached = jnp.where(valid[:, None, None, :], cached, -jnp.inf)
    local = (
        jnp.einsum("rcgd,red->rgce", heads_q, block_keys, preferred_element_type=jnp.float32)
        * scale
    )
    causal = jnp.arange(steps)[:, None] >= jnp.arange(steps)[None, :]
    local = jnp.where(causal[None, None], local, -jnp.inf)
    top = jnp.maximum(jnp.max(cached, axis=-1), jnp.max(local, axis=-1))
    exp_cached = jnp.exp(cached - top[..., None])
    exp_local = jnp.exp(local - top[..., None])
    total = jnp.sum(exp_cached, axis=-1) + jnp.sum(exp_local, axis=-1)
    w_cached = (exp_cached / total[..., None]).astype(jnp.bfloat16)
    w_local = (exp_local / total[..., None]).astype(jnp.bfloat16)
    result = jnp.einsum("rgcp,rpd->rcgd", w_cached, cache_vals, preferred_element_type=jnp.float32)
    result = result + jnp.einsum(
        "rgce,red->rcgd", w_local, block_vals, preferred_element_type=jnp.float32
    )
    return result.reshape(req_count * steps, width).astype(jnp.bfloat16)


def shards(queries, block_kv, cache_kv, prefix_len, residual, out_weight):
    attended = attend_local(queries, block_kv, cache_kv, prefix_len)
    partial_value = jnp.dot(
        lax.all_gather(attended, "sub", axis=0, tiled=True),
        out_weight,
        preferred_element_type=jnp.float32,
    ).astype(jnp.bfloat16)
    terms = lax.optimization_barrier(partial_value).astype(jnp.float32)
    summed = lax.psum_scatter(terms, "tp", scatter_dimension=0, tiled=True)
    stream_rows = (residual.astype(jnp.float32) + summed).astype(jnp.bfloat16)
    return lax.all_gather(stream_rows, "tp", axis=0, tiled=True)


def solution(mesh):
    in_specs = (
        P(("groups", "sub"), None, "tp"),
        P(("groups", "sub"), None, None, "tp"),
        P(("groups", "sub"), None, "tp", None, None),
        P(("groups", "sub")),
        P(("groups", "tp"), "sub"),
        P("tp", "sub"),
    )
    out_specs = P("groups", "sub")
    return jax.shard_map(shards, mesh=mesh, in_specs=in_specs, out_specs=out_specs, check_vma=False)
```

profile of v0, /device:TPU:0, one launch (start us, length us, event | category | flops | bytes accessed | tf_op | source)
XLA Modules:
  0.0 197.4 jit_solution(11942973957358653933)
XLA Ops:
  6.5 0.0 all-gather.3.cloned.1.call-start
  7.2 0.9 fusion.20
  8.1 1.1 copy.21
  9.3 0.6 fusion.21
  9.9 0.0 copy-start.1
  9.9 2.4 %bitcast_reduce_fusion = (f32[32,64]{1,0:T(8,128)S(1)}, f32[1024,64,32]{0,1,2:T(8,128)S(1)}) fusion(pred[1024]{0:T(1024)(128)(4,1)S(1)} %iota_compare_fusion.1, bf16[64,32,128]{2,1,0:T(8,128)(2,1)S(1)} %bitcast.80, bf16[1,2,1,1024,128]{4,3,2,1,0:T(8,128)(2,1)} %param.8), kind=kOutput, calls=%fused_computation.1 | convolution fusion | flops 543160320 | bytes 9184256 | tf_op jit(solution)/shard_map/rcgd,rpd->rgcp/dot_general | solution.py:20
  12.4 0.2 fusion.8
  12.6 2.0 %fusion.1 = f32[32,64]{1,0:T(8,128)S(1)} fusion(f32[1024,64,32]{0,1,2:T(8,128)S(1)} %get-tuple-element.8, f32[32,64]{1,0:T(8,128)S(1)} %max.9, pred[1024]{0:T(1024)(128)(4,1)S(1)} %iota_compare_fusion.1), kind=kLoop, calls=%fused_computation.5 | loop fusion | flops 8386560 | bytes 8406016 | tf_op jit(solution)/shard_map/reduce_sum | solution.py:34
  14.6 0.0 copy-done.1
  14.6 2.2 %fusion.2 = f32[32,64,128]{2,1,0:T(8,128)S(1)} fusion(f32[1024,64,32]{0,1,2:T(8,128)S(1)} %get-tuple-element.8, f32[32,64]{1,0:T(8,128)S(1)} %add.20, f32[32,64]{1,0:T(8,128)S(1)} %max.9, pred[1024]{0:T(1024)(128)(4,1)S(1)} %iota_compare_fusion.1, bf16[1,2,1,1024,128]{4,3,2,1,0:T(8,128)(2,1)S(1)} %copy-done.1), kind=kOutput, calls=%fused_computation.7 | convolution fusion | flops 547356672 | bytes 9733120 | tf_op jit(solution)/shard_map/rgcp,rpd->rcgd/dot_general | solution.py:37
  16.8 0.4 fusion.7
  17.1 0.3 copy.17
  17.5 1.0 copy.38
  18.5 0.0 all-gather.3.cloned.1.call-update
  18.5 0.0 reduce-scatter.2.cloned.1.call-start
  18.6 25.4 %all-gather.3.cloned.1.call-done = bf16[256,4096]{1,0:T(8,128)(2,1)} async-done(((bf16[64,4096]{1,0:T(8,128)(2,1)}), bf16[256,4096]{1,0:T(8,128)(2,1)}) %all-gather.3.cloned.1.call-update) | async-done | bytes 2097168 | tf_op jit(solution)/shard_map/all_gather | solution.py:47
  44.0 15.6 %convolution_convert_fusion = bf16[256,4096]{1,0:T(8,128)(2,1)S(1)} fusion(bf16[256,4096]{1,0:T(8,128)(2,1)} %all-gather.3.cloned.1.call-done, bf16[4096,4096]{1,0:T(8,128)(2,1)} %param.11), kind=kOutput, calls=%fused_computation.6 | convolution fusion | flops 8590983168 | bytes 37748736 | tf_op jit(solution)/shard_map/dot_general | solution.py:46
  59.6 0.0 copy-start
  59.6 2.4 %convert_element_type.42 = f32[256,4096]{1,0:T(8,128)} convert(bf16[256,4096]{1,0:T(8,128)(2,1)S(1)} %convolution_convert_fusion) | non-fusion elementwise | flops 1048576 | bytes 6291456 | tf_op jit(solution)/shard_map/convert_element_type | solution.py:51
  62.0 0.0 reduce-scatter.2.cloned.1.call-update
  62.1 0.0 all-gather.5.cloned.1.call-start
  62.1 76.9 %reduce-scatter.2.cloned.1.call-done = f32[64,4096]{1,0:T(8,128)} async-done(((f32[256,4096]{1,0:T(8,128)}), f32[64,4096]{1,0:T(8,128)}) %reduce-scatter.2.cloned.1.call-update) | async-done | bytes 1048592 | tf_op jit(solution)/shard_map/reduce_scatter | solution.py:52
  139.0 0.0 copy-done
  139.0 2.1 %add_convert_fusion = bf16[64,4096]{1,0:T(8,128)(2,1)} fusion(f32[64,4096]{1,0:T(8,128)} %reduce-scatter.2.cloned.1.call-done, bf16[64,4096]{1,0:T(8,128)(2,1)S(1)} %copy-done), kind=kLoop, calls=%fused_computation.15 | loop fusion | flops 786432 | bytes 2097152 | tf_op jit(solution)/shard_map/convert_element_type | solution.py:53
  141.1 0.0 all-gather.5.cloned.1.call-update
  141.1 46.6 %all-gather.5.cloned.1.call-done = bf16[256,4096]{1,0:T(8,128)(2,1)} async-done(((bf16[64,4096]{1,0:T(8,128)(2,1)}), bf16[256,4096]{1,0:T(8,128)(2,1)}) %all-gather.5.cloned.1.call-update) | async-done | bytes 2097168 | tf_op jit(solution)/shard_map/all_gather | solution.py:54
  187.7 3.1 %copy.41 = bf16[256,4096]{1,0:T(8,128)(2,1)} copy(bf16[256,4096]{1,0:T(8,128)(2,1)} %all-gather.5.cloned.1.call-done) | data formatting | bytes 4194304
  (4 shorter events, 0.0 us)
Async XLA Ops:
  6.5 37.4 %all-gather.3.cloned.1.call-start = ((), (), s32[]{:S(2)}) async-start(), calls=%async_computation.1 | async-start | bytes 2621440 | tf_op jit(solution)/shard_map/all_gather | solution.py:47
  9.9 4.7 %copy-start.1 = (bf16[1,2,1,1024,128]{4,3,2,1,0:T(8,128)(2,1)S(1)}, bf16[1,2,1,1024,128]{4,3,2,1,0:T(8,128)(2,1)}, u32[]{:S(2)}) copy-start(bf16[1,2,1,1024,128]{4,3,2,1,0:T(8,128)(2,1)} %param.8) | copy-start | bytes 1572868
  18.5 120.5 %reduce-scatter.2.cloned.1.call-start = ((), (), s32[]{:S(2)}) async-start(), calls=%async_computation.2 | async-start | bytes 5242880 | tf_op jit(solution)/shard_map/reduce_scatter | solution.py:52
  59.6 79.4 %copy-start = (bf16[64,4096]{1,0:T(8,128)(2,1)S(1)}, bf16[64,4096]{1,0:T(8,128)(2,1)}, u32[]{:S(2)}) copy-start(bf16[64,4096]{1,0:T(8,128)(2,1)} %param.10) | copy-start | bytes 1572868
  62.1 125.7 %all-gather.5.cloned.1.call-start = ((), (), s32[]{:S(2)}) async-start(), calls=%async_computation.3 | async-start | bytes 2621440 | tf_op jit(solution)/shard_map/all_gather | solution.py:54
Sparse Core Ops, SparseCore 0:
  18.6 25.2 all-gather.2
  62.2 76.7 reduce-scatter.1
  141.2 46.4 all-gather.4
where the time goes:
time: 198 us; the launch traced here: 197 us
  waiting for transfers between devices  149 us (75%)
  matrix products  21.2 us (11%)
  between operations  13.9 us (7%)
  other arithmetic  6.74 us (3%)
  local copies, waits for them, and re-layouts  6.52 us (3%)
    reduce_scatter x1, waiting for transfers between devices, shards(): summed = lax.psum_scatter(terms, 'tp', scatter_dimension=0, tiled=True)  76.9 us
    all_gather x1, waiting for transfers between devices, shards(): return lax.all_gather(stream_rows, 'tp', axis=0, tiled=True)  46.6 us
    all_gather x1, waiting for transfers between devices, shards(): lax.all_gather(attended, 'sub', axis=0, tiled=True)  25.4 us
    dot_general x1, matrix products, shards(): jnp.dot(lax.all_gather(attended, 'sub', axis=0, tiled=True), out_weight,...  15.6 us
    unnamed x7, local copies, waits for them, and re-layouts  5.28 us
  transfers between devices with their start and end apart: 3, of which 3 were waited for; matrix products, arithmetic and copies ran while one was open for 0% of the time, Pallas kernels for 0%

commit v1 on v0

--- a/solution.py
+++ b/solution.py
@@ -1,6 +1,8 @@
 import jax
 import jax.numpy as jnp
 from jax import lax
+from jax.experimental import pallas as pl
+from jax.experimental.pallas import tpu as pltpu
 from jax.sharding import PartitionSpec as P
 
 HD = 128
@@ -54,6 +56,223 @@
     return lax.all_gather(stream_rows, "tp", axis=0, tiled=True)
 
 
+TP_LINE, SUB_RING = 4, 4
+TILE, LAG = 512, 2
+MESH = pl.DeviceIdType.MESH
+
+
+def mix_kernel(att, res, w, out, rows, wv, acc, snd, rin, xin, tot, wsem, gsem, grcv, asem, esem, isem, tsem, tend, osem):
+    t, s = lax.axis_index("tp"), lax.axis_index("sub")
+    core, chip = s % 2, s // 2
+    sibling, across = chip * 2 + 1 - core, (1 - chip) * 2 + core
+    edge = (t == 0) | (t == TP_LINE - 1)
+    inner = (t == 1) | (t == 2)
+    side = t // 2
+    inward = 1 + side
+    outward = side * 3
+    opposite = 3 - t
+    block = att.shape[0]
+    tiles = wv.shape[0]
+    chunks = 2 * tiles
+
+    def load(j):
+        return pltpu.make_async_copy(w.at[:, pl.ds(pl.multiple_of(j * TILE, TILE), TILE)], wv.at[j], wsem.at[j])
+
+    def start_load(j, carry):
+        load(j).start()
+        return carry
+
+    lax.fori_loop(0, tiles, start_load, 0)
+
+    barrier = pltpu.get_barrier_semaphore()
+    for peer in (sibling, across):
+        pl.semaphore_signal(barrier, inc=1, device_id={"sub": peer}, device_id_type=MESH)
+
+    @pl.when(edge)
+    def _():
+        pl.semaphore_signal(barrier, inc=1, device_id={"tp": inward}, device_id_type=MESH)
+        pl.semaphore_wait(barrier, 3)
+
+    @pl.when(inner)
+    def _():
+        pl.semaphore_signal(barrier, inc=1, device_id={"tp": outward}, device_id_type=MESH)
+        pl.semaphore_signal(barrier, inc=1, device_id={"tp": opposite}, device_id_type=MESH)
+        pl.semaphore_wait(barrier, 4)
+
+    mine = pl.ds(pl.multiple_of(core * block, block), block)
+
+    def gather(src, slot, n, peer):
+        return pltpu.make_async_remote_copy(
+            src_ref=src, dst_ref=rows.at[slot, mine], send_sem=gsem.at[n], recv_sem=grcv.at[n],
+            device_id={"sub": peer}, device_id_type=MESH,
+        )
+
+    to_sibling = gather(att, 0, 0, sibling)
+    to_across = gather(att, 1, 1, across)
+    forward = gather(rows.at[1, mine], 1, 2, sibling)
+    to_across.start()
+    to_sibling.start()
+    rows[0, mine, :] = att[...]
+    to_sibling.wait_recv()
+
+    def send(src, dst, n, out_sem, in_sem, peer):
+        return pltpu.make_async_remote_copy(
+            src_ref=src.at[n], dst_ref=dst.at[n], send_sem=out_sem.at[n], recv_sem=in_sem.at[n],
+            device_id={"tp": peer}, device_id_type=MESH,
+        )
+
+    def from_edge(n):
+        return send(snd, rin, n, asem, esem, inward)
+
+    def to_opposite(n):
+        return send(snd, xin, n, asem, isem, opposite)
+
+    def to_edge(n):
+        return send(tot, tot, n, tsem, tend, outward)
+
+    def store(n):
+        phase, j = n // tiles, n % tiles
+        part = chip + phase - 2 * chip * phase
+        return pltpu.make_async_copy(
+            tot.at[n],
+            out.at[
+                pl.ds(pl.multiple_of(part * 2 * block, 2 * block), 2 * block),
+                pl.ds(pl.multiple_of(j * TILE, TILE), TILE),
+            ],
+            osem.at[n],
+        )
+
+    def finish(n):
+        to_opposite(n).wait_recv()
+        total = snd[n].astype(jnp.float32) + xin[n].astype(jnp.float32)
+        tot[n] = total.astype(tot.dtype)
+        to_edge(n).start()
+        store(n).start()
+
+    def step(n, carry):
+        phase, j = n // tiles, n % tiles
+        part = chip + phase - 2 * chip * phase
+
+        @pl.when(phase == 0)
+        def _():
+            load(j).wait()
+
+        @pl.when(n == tiles // 2)
+        def _():
+            to_across.wait_recv()
+            forward.start()
+
+        @pl.when(n == tiles)
+        def _():
+            forward.wait_recv()
+
+        acc[...] = jnp.dot(rows[phase], wv[j], preferred_element_type=jnp.float32)
+
+        @pl.when(side == part)
+        def _():
+            at = pl.ds(pl.multiple_of((t % 2) * block, block), block)
+            acc[at, :] += res[:, pl.ds(pl.multiple_of(j * TILE, TILE), TILE)].astype(jnp.float32)
+
+        @pl.when(edge)
+        def _():
+            snd[n] = acc[...].astype(snd.dtype)
+            from_edge(n).start()
+
+        @pl.when(inner)
+        def _():
+            from_edge(n).wait_recv()
+            snd[n] = (acc[...] + rin[n].astype(jnp.float32)).astype(snd.dtype)
+            to_opposite(n).start()
+
+        @pl.when(inner & (n >= LAG))
+        def _():
+            finish(n - LAG)
+
+        return carry
+
+    lax.fori_loop(0, chunks, step, 0)
+
+    @pl.when(inner)
+    def _():
+        def rest(n, carry):
+            finish(n)
+            return carry
+
+        lax.fori_loop(chunks - LAG, chunks, rest, 0)
+
+        def drain(n, carry):
+            to_opposite(n).wait_send()
+            to_edge(n).wait_send()
+            store(n).wait()
+            return carry
+
+        lax.fori_loop(0, chunks, drain, 0)
+
+    @pl.when(edge)
+    def _():
+        def take(n, carry):
+            to_edge(n).wait_recv()
+            store(n).start()
+            return carry
+
+        lax.fori_loop(0, chunks, take, 0)
+
+        def drain(n, carry):
+            from_edge(n).wait_send()
+            store(n).wait()
+            return carry
+
+        lax.fori_loop(0, chunks, drain, 0)
+
+    to_sibling.wait_send()
+    to_across.wait_send()
+    forward.wait_send()
+
+
+def mix(attended, residual, out_weight):
+    block, depth = attended.shape
+    width = out_weight.shape[1]
+    tiles = width // TILE
+    chunks = 2 * tiles
+    dma = pltpu.SemaphoreType.DMA
+    chunk_buffer = pltpu.VMEM((chunks, 2 * block, TILE), jnp.bfloat16)
+    return pl.pallas_call(
+        mix_kernel,
+        out_shape=jax.ShapeDtypeStruct((4 * block, width), jnp.bfloat16),
+        in_specs=[
+            pl.BlockSpec(memory_space=pltpu.VMEM),
+            pl.BlockSpec(memory_space=pltpu.VMEM),
+            pl.BlockSpec(memory_space=pl.ANY),
+        ],
+        out_specs=pl.BlockSpec(memory_space=pl.ANY),
+        scratch_shapes=[
+            pltpu.VMEM((2, 2 * block, depth), jnp.bfloat16),
+            pltpu.VMEM((tiles, depth, TILE), jnp.bfloat16),
+            pltpu.VMEM((2 * block, TILE), jnp.float32),
+            chunk_buffer,
+            chunk_buffer,
+            chunk_buffer,
+            chunk_buffer,
+            dma((tiles,)),
+            dma((3,)),
+            dma((3,)),
+            dma((chunks,)),
+            dma((chunks,)),
+            dma((chunks,)),
+            dma((chunks,)),
+            dma((chunks,)),
+            dma((chunks,)),
+        ],
+        compiler_params=pltpu.CompilerParams(
+            collective_id=0, has_side_effects=True, vmem_limit_bytes=52 * 1024 * 1024
+        ),
+    )(attended, residual, out_weight)
+
+
+def line_shards(queries, block_kv, cache_kv, prefix_len, residual, out_weight):
+    return mix(attend_local(queries, block_kv, cache_kv, prefix_len), residual, out_weight)
+
+
 def solution(mesh):
     in_specs = (
         P(("groups", "sub"), None, "tp"),
@@ -64,4 +283,6 @@
         P("tp", "sub"),
     )
     out_specs = P("groups", "sub")
-    return jax.shard_map(shards, mesh=mesh, in_specs=in_specs, out_specs=out_specs, check_vma=False)
+    fits = mesh.shape["tp"] == TP_LINE and mesh.shape["sub"] == SUB_RING
+    body = line_shards if fits else shards
+    return jax.shard_map(body, mesh=mesh, in_specs=in_specs, out_specs=out_specs, check_vma=False)

time: 198 us -> 79.9 us (0.40)
  waiting for transfers between devices: 149 us -> 0 us
  Pallas kernels: 0 us -> 65.4 us
  matrix products: 21.2 us -> 5.54 us
  between operations: 13.9 us -> 0.79 us
  other arithmetic: 6.74 us -> 2.15 us
    reduce_scatter x1 -> x0, waiting for transfers between devices: 76.9 us -> none  [shards(): summed = lax.psum_scatter(terms, 'tp', scatter_dimension=0, tiled=True)]
    all_gather x2 -> x0, waiting for transfers between devices: 72 us -> none  [the longest x1 46.6 us: shards(): return lax.all_gather(stream_rows, 'tp', axis=0, tiled=True)]
    pallas_call x0 -> x1, Pallas kernels: none -> 65.4 us  [mix(): pl.pallas_call(mix_kernel, out_shape=jax.ShapeDtypeStruct((4 * block, wid...]
    dot_general x1 -> x0, matrix products: 15.6 us -> none  [shards(): jnp.dot(lax.all_gather(attended, 'sub', axis=0, tiled=True), out_weight,...]
    convert_element_type x2 -> x0, other arithmetic: 4.52 us -> none  [the longest x1 2.41 us: shards(): terms = lax.optimization_barrier(partial_value).astype(jnp.float32)]
  transfers between devices with their start and end apart: 3 -> 0, of which waited for: 3 -> 0; matrix products, arithmetic and copies ran while one was open for 0% -> 0% of each run, Pallas kernels for 0% -> 0%
where the time goes in v1:
time: 79.9 us; the launch traced here: 79.6 us
  Pallas kernels  65.4 us (82%)
  local copies, waits for them, and re-layouts  5.73 us (7%)
  matrix products  5.54 us (7%)
  other arithmetic  2.15 us (3%)
    pallas_call x1, Pallas kernels, mix(): pl.pallas_call(mix_kernel, out_shape=jax.ShapeDtypeStruct((4 * block, wid...  65.4 us
    unnamed x7, local copies, waits for them, and re-layouts  4.49 us
    dot_general x1, matrix products, attend_local(): jnp.einsum('rcgd,rpd->rgcp', heads_q, cache_keys, preferred_element_type=...  2.42 us
    reduce_sum x2, other arithmetic, attend_local(): total = jnp.sum(exp_cached, axis=-1) + jnp.sum(exp_local, axis=-1)  2.13 us
    dot_general x1, matrix products, attend_local(): jnp.einsum('rgcp,rpd->rcgd', w_cached, cache_vals, preferred_element_type...  2.11 us

profile of v1, /device:TPU:0, one launch (start us, length us, event | category | flops | bytes accessed | tf_op | source)
XLA Modules:
  0.0 79.6 jit_solution(375784367768032747)
XLA Ops:
  0.7 0.9 %fusion.20 = (bf16[1,64,1,128]{3,2,1,0:T(2,128)(2,1)S(1)}, bf16[1,64,1,128]{3,2,1,0:T(2,128)(2,1)S(1)}) fusion(bf16[1,64,2,128]{3,2,1,0:T(2,128)(2,1)} %param.7), kind=kLoop, calls=%fused_computation.33 | loop fusion | bytes 65536 | tf_op jit(solution)/shard_map/slice | solution.py:17
  1.6 1.1 %copy.16 = bf16[8,8,32,128]{3,2,1,0:T(8,128)(2,1)S(1)} copy(bf16[8,8,32,128]{3,1,2,0:T(8,128)(2,1)} %bitcast.81) | data formatting | bytes 1048576
  2.7 0.6 fusion.21
  3.4 0.0 copy-start.1
  3.4 2.4 %bitcast_reduce_fusion = (f32[32,64]{1,0:T(8,128)S(1)}, f32[1024,64,32]{0,1,2:T(8,128)S(1)}) fusion(pred[1024]{0:T(1024)(128)(4,1)S(1)} %iota_compare_fusion.1, bf16[64,32,128]{2,1,0:T(8,128)(2,1)S(1)} %bitcast.79, bf16[1,2,1,1024,128]{4,3,2,1,0:T(8,128)(2,1)} %param.8), kind=kOutput, calls=%fused_computation.1 | convolution fusion | flops 543160320 | bytes 9184256 | tf_op jit(solution)/shard_map/rcgd,rpd->rgcp/dot_general | solution.py:22
  5.8 0.2 fusion.8
  6.1 1.9 %fusion.1 = f32[32,64]{1,0:T(8,128)S(1)} fusion(f32[1024,64,32]{0,1,2:T(8,128)S(1)} %get-tuple-element.8, f32[32,64]{1,0:T(8,128)S(1)} %max.9, pred[1024]{0:T(1024)(128)(4,1)S(1)} %iota_compare_fusion.1), kind=kLoop, calls=%fused_computation.5 | loop fusion | flops 8386560 | bytes 8406016 | tf_op jit(solution)/shard_map/reduce_sum | solution.py:36
  8.0 0.0 copy-done.1
  8.0 0.0 copy-start
  8.0 2.1 %fusion.2 = f32[32,64,128]{2,1,0:T(8,128)S(1)} fusion(f32[1024,64,32]{0,1,2:T(8,128)S(1)} %get-tuple-element.8, f32[32,64]{1,0:T(8,128)S(1)} %add.15, f32[32,64]{1,0:T(8,128)S(1)} %max.9, pred[1024]{0:T(1024)(128)(4,1)S(1)} %iota_compare_fusion.1, bf16[1,2,1,1024,128]{4,3,2,1,0:T(8,128)(2,1)S(1)} %copy-done.1), kind=kOutput, calls=%fused_computation.6 | convolution fusion | flops 547356672 | bytes 9733120 | tf_op jit(solution)/shard_map/rgcp,rpd->rcgd/dot_general | solution.py:39
  10.1 0.4 fusion.7
  10.5 0.3 copy.12
  10.8 0.2 copy.33
  11.1 0.0 copy-done
  11.1 65.4 %shard_map.64 = bf16[256,4096]{1,0:T(8,128)(2,1)} custom-call(bf16[64,4096]{1,0:T(8,128)(2,1)S(1)} %bitcast.77, bf16[64,4096]{1,0:T(8,128)(2,1)S(1)} %copy-done, bf16[4096,4096]{1,0:T(8,128)(2,1)} %w.1), custom_call_target="tpu_custom_call" | custom-call | tf_op jit(solution)/shard_map/pallas_call | solution.py:239
  76.5 3.1 %copy.36 = bf16[256,4096]{1,0:T(8,128)(2,1)} copy(bf16[256,4096]{1,0:T(8,128)(2,1)} %shard_map.64) | data formatting | bytes 4194304
  (4 shorter events, 0.0 us)
Async XLA Ops:
  3.4 4.6 %copy-start.1 = (bf16[1,2,1,1024,128]{4,3,2,1,0:T(8,128)(2,1)S(1)}, bf16[1,2,1,1024,128]{4,3,2,1,0:T(8,128)(2,1)}, u32[]{:S(2)}) copy-start(bf16[1,2,1,1024,128]{4,3,2,1,0:T(8,128)(2,1)} %param.8) | copy-start | bytes 1572868
  8.0 3.1 %copy-start = (bf16[64,4096]{1,0:T(8,128)(2,1)S(1)}, bf16[64,4096]{1,0:T(8,128)(2,1)}, u32[]{:S(2)}) copy-start(bf16[64,4096]{1,0:T(8,128)(2,1)} %res.1) | copy-start | bytes 1572868

commit v2 on v1

--- a/solution.py
+++ b/solution.py
@@ -57,11 +57,16 @@
 
 
 TP_LINE, SUB_RING = 4, 4
-TILE, LAG = 512, 2
+TILE, LAG = 256, 2
+HEADS_AT_ONCE = 4
+LOG2E = 1.4426950408889634
 MESH = pl.DeviceIdType.MESH
 
 
-def mix_kernel(att, res, w, out, rows, wv, acc, snd, rin, xin, tot, wsem, gsem, grcv, asem, esem, isem, tsem, tend, osem):
+def mix_kernel(
+    lens, queries, new_kv, cache, res, w, out, qv, bv, cv, rows, wv, acc, snd, rin, xin, tot,
+    qsem, wsem, psem, prcv, gsem, grcv, asem, esem, isem, tsem, tend, osem,
+):
     t, s = lax.axis_index("tp"), lax.axis_index("sub")
     core, chip = s % 2, s // 2
     sibling, across = chip * 2 + 1 - core, (1 - chip) * 2 + core
@@ -71,7 +76,9 @@
     inward = 1 + side
     outward = side * 3
     opposite = 3 - t
-    block = att.shape[0]
+    block = res.shape[0]
+    span = HEADS_AT_ONCE * HD
+    groups = qv.shape[1] // span
     tiles = wv.shape[0]
     chunks = 2 * tiles
 
@@ -82,6 +89,12 @@
         load(j).start()
         return carry
 
+    first = [
+        pltpu.make_async_copy(src, dst, qsem.at[n])
+        for n, (src, dst) in enumerate(((queries, qv), (new_kv, bv), (cache, cv)))
+    ]
+    for copy in first:
+        copy.start()
     lax.fori_loop(0, tiles, start_load, 0)
 
     barrier = pltpu.get_barrier_semaphore()
@@ -91,29 +104,72 @@
     @pl.when(edge)
     def _():
         pl.semaphore_signal(barrier, inc=1, device_id={"tp": inward}, device_id_type=MESH)
-        pl.semaphore_wait(barrier, 3)
 
     @pl.when(inner)
     def _():
         pl.semaphore_signal(barrier, inc=1, device_id={"tp": outward}, device_id_type=MESH)
         pl.semaphore_signal(barrier, inc=1, device_id={"tp": opposite}, device_id_type=MESH)
-        pl.semaphore_wait(barrier, 4)
 
     mine = pl.ds(pl.multiple_of(core * block, block), block)
 
-    def gather(src, slot, n, peer):
+    def piece(n):
+        part_of_row = rows.at[0, mine, pl.ds(pl.multiple_of(n * span, span), span)]
         return pltpu.make_async_remote_copy(
-            src_ref=src, dst_ref=rows.at[slot, mine], send_sem=gsem.at[n], recv_sem=grcv.at[n],
+            src_ref=part_of_row, dst_ref=part_of_row, send_sem=psem.at[n], recv_sem=prcv.at[n],
+            device_id={"sub": sibling}, device_id_type=MESH,
+        )
+
+    def gather(slot, n, peer):
+        return pltpu.make_async_remote_copy(
+            src_ref=rows.at[slot, mine], dst_ref=rows.at[1, mine], send_sem=gsem.at[n], recv_sem=grcv.at[n],
             device_id={"sub": peer}, device_id_type=MESH,
         )
 
-    to_sibling = gather(att, 0, 0, sibling)
-    to_across = gather(att, 1, 1, across)
-    forward = gather(rows.at[1, mine], 1, 2, sibling)
+    to_across = gather(0, 0, across)
+    forward = gather(1, 1, sibling)
+
+    for copy in first:
+        copy.wait()
+    capacity = cv.shape[1]
+    held = lax.broadcasted_iota(jnp.int32, (1, capacity), 1) < lens[0]
+    bias = jnp.where(held, 0.0, -jnp.inf).astype(jnp.float32)
+    many = HEADS_AT_ONCE * block
+    token = lax.rem(lax.broadcasted_iota(jnp.int32, (many, block), 0), block)
+    causal = token >= lax.broadcasted_iota(jnp.int32, (many, block), 1)
+    factor = HD ** (-0.5) * LOG2E
+    last = (((1,), (1,)), ((), ()))
+
+    def attend(n, carry):
+        wide = qv[:, pl.ds(pl.multiple_of(n * span, span), span)]
+        q = jnp.concatenate([wide[:, i * HD : (i + 1) * HD] for i in range(HEADS_AT_ONCE)], axis=0)
+        old = lax.dot_general(q, cv[0], last, preferred_element_type=jnp.float32) + bias
+        new = lax.dot_general(q, bv[:, :HD], last, preferred_element_type=jnp.float32)
+        new = jnp.where(causal, new, -jnp.inf)
+        top = jnp.maximum(jnp.max(old, axis=1, keepdims=True), jnp.max(new, axis=1, keepdims=True))
+        old = jnp.exp2((old - top) * factor)
+        new = jnp.exp2((new - top) * factor)
+        part = 1.0 / (jnp.sum(old, axis=1, keepdims=True) + jnp.sum(new, axis=1, keepdims=True))
+        got = jnp.dot((old * part).astype(jnp.bfloat16), cv[1], preferred_element_type=jnp.float32)
+        got += jnp.dot((new * part).astype(jnp.bfloat16), bv[:, HD:], preferred_element_type=jnp.float32)
+        for i in range(HEADS_AT_ONCE):
+            at = pl.ds(pl.multiple_of(n * span + i * HD, HD), HD)
+            rows[0, mine, at] = got[i * block : (i + 1) * block].astype(jnp.bfloat16)
+
+        @pl.when(n == 0)
+        def _():
+            pl.semaphore_wait(barrier, jnp.where(edge, 3, 4))
+
+        piece(n).start()
+        return carry
+
+    lax.fori_loop(0, groups, attend, 0)
     to_across.start()
-    to_sibling.start()
-    rows[0, mine, :] = att[...]
-    to_sibling.wait_recv()
+
+    def take_piece(n, carry):
+        piece(n).wait_recv()
+        return carry
+
+    lax.fori_loop(0, groups, take_piece, 0)
 
     def send(src, dst, n, out_sem, in_sem, peer):
         return pltpu.make_async_remote_copy(
@@ -224,28 +280,40 @@
 
         lax.fori_loop(0, chunks, drain, 0)
 
-    to_sibling.wait_send()
+    def drain_piece(n, carry):
+        piece(n).wait_send()
+        return carry
+
+    lax.fori_loop(0, groups, drain_piece, 0)
     to_across.wait_send()
     forward.wait_send()
 
 
-def mix(attended, residual, out_weight):
-    block, depth = attended.shape
+def line_shards(queries, block_kv, cache_kv, prefix_len, residual, out_weight):
+    block, depth = queries.shape[1:]
     width = out_weight.shape[1]
     tiles = width // TILE
     chunks = 2 * tiles
+    groups = depth // (HEADS_AT_ONCE * HD)
     dma = pltpu.SemaphoreType.DMA
     chunk_buffer = pltpu.VMEM((chunks, 2 * block, TILE), jnp.bfloat16)
+    anywhere = pl.BlockSpec(memory_space=pl.ANY)
     return pl.pallas_call(
         mix_kernel,
         out_shape=jax.ShapeDtypeStruct((4 * block, width), jnp.bfloat16),
         in_specs=[
+            pl.BlockSpec(memory_space=pltpu.SMEM),
+            anywhere,
+            anywhere,
+            anywhere,
             pl.BlockSpec(memory_space=pltpu.VMEM),
-            pl.BlockSpec(memory_space=pltpu.VMEM),
-            pl.BlockSpec(memory_space=pl.ANY),
+            anywhere,
         ],
-        out_specs=pl.BlockSpec(memory_space=pl.ANY),
+        out_specs=anywhere,
         scratch_shapes=[
+            pltpu.VMEM((block, depth), jnp.bfloat16),
+            pltpu.VMEM((block, 2 * HD), jnp.bfloat16),
+            pltpu.VMEM((2,) + cache_kv.shape[3:], jnp.bfloat16),
             pltpu.VMEM((2, 2 * block, depth), jnp.bfloat16),
             pltpu.VMEM((tiles, depth, TILE), jnp.bfloat16),
             pltpu.VMEM((2 * block, TILE), jnp.float32),
@@ -253,9 +321,12 @@
             chunk_buffer,
             chunk_buffer,
             chunk_buffer,
+            dma((3,)),
             dma((tiles,)),
-            dma((3,)),
-            dma((3,)),
+            dma((groups,)),
+            dma((groups,)),
+            dma((2,)),
+            dma((2,)),
             dma((chunks,)),
             dma((chunks,)),
             dma((chunks,)),
@@ -264,13 +335,16 @@
             dma((chunks,)),
         ],
         compiler_params=pltpu.CompilerParams(
-            collective_id=0, has_side_effects=True, vmem_limit_bytes=52 * 1024 * 1024
+            collective_id=0, has_side_effects=True, vmem_limit_bytes=56 * 1024 * 1024
         ),
-    )(attended, residual, out_weight)
-
-
-def line_shards(queries, block_kv, cache_kv, prefix_len, residual, out_weight):
-    return mix(attend_local(queries, block_kv, cache_kv, prefix_len), residual, out_weight)
+    )(
+        prefix_len,
+        queries.reshape(block, depth),
+        block_kv.reshape(block, 2 * HD),
+        cache_kv.reshape((2,) + cache_kv.shape[3:]),
+        residual,
+        out_weight,
+    )
 
 
 def solution(mesh):

time: 79.9 us -> 77.4 us (0.969)
  Pallas kernels: 65.4 us -> 72 us
  matrix products: 5.54 us -> 0 us
  other arithmetic: 2.15 us -> 0 us
  local copies, waits for them, and re-layouts: 5.73 us -> 4.51 us
    pallas_call x1, Pallas kernels: 65.4 us -> 72 us  [line_shards(): pl.pallas_call(mix_kernel, out_shape=jax.ShapeDtypeStruct((4 * block, wid...]
    dot_general x4 -> x0, matrix products: 5.54 us -> none  [the longest x1 2.42 us: attend_local(): jnp.einsum('rcgd,rpd->rgcp', heads_q, cache_keys, preferred_element_type=...]
    reduce_sum x2 -> x0, other arithmetic: 2.13 us -> none  [attend_local(): total = jnp.sum(exp_cached, axis=-1) + jnp.sum(exp_local, axis=-1)]
    slice x1 -> x0, local copies, waits for them, and re-layouts: 0.89 us -> none  [attend_local(): block_vals = block_kv[:, :, 1, :]]
    unnamed x7 -> x2, local copies, waits for them, and re-layouts: 4.49 us -> 4.51 us
where the time goes in v2:
time: 77.4 us; the launch traced here: 77.2 us
  Pallas kernels  72 us (93%)
  local copies, waits for them, and re-layouts  4.51 us (6%)
    pallas_call x1, Pallas kernels, line_shards(): pl.pallas_call(mix_kernel, out_shape=jax.ShapeDtypeStruct((4 * block, wid...  72 us
    unnamed x2, local copies, waits for them, and re-layouts  4.51 us

profile of v2, /device:TPU:0, one launch (start us, length us, event | category | flops | bytes accessed | tf_op | source)
XLA Modules:
  0.0 77.2 jit_solution(11060044335265558827)
XLA Ops:
  0.7 1.4 %copy.9 = bf16[8,8,2,128]{3,1,2,0:T(8,128)(2,1)} copy(bf16[8,8,2,128]{3,2,1,0:T(2,128)(2,1)} %bitcast.10) | data formatting | bytes 65536
  2.0 72.0 %shard_map.64 = bf16[256,4096]{1,0:T(8,128)(2,1)} custom-call(s32[1]{0:T(128)S(6)} %copy.11.lens, bf16[64,4096]{1,0:T(8,128)(2,1)} %bitcast.7, bf16[64,256]{1,0:T(8,128)(2,1)} %bitcast.9, bf16[2,1024,128]{2,1,0:T(8,128)(2,1)} %bitcast.8, bf16[64,4096]{1,0:T(8,128)(2,1)} %res.1, bf16[4096,4096]{1,0:T(8,128)(2,1)} %w.1), custom_call_target="tpu_custom_call" | custom-call | tf_op jit(solution)/shard_map/pallas_call | solution.py:301
  74.0 3.1 %copy.12 = bf16[256,4096]{1,0:T(8,128)(2,1)} copy(bf16[256,4096]{1,0:T(8,128)(2,1)} %shard_map.64) | data formatting | bytes 4194304

commit v3 on v2

--- a/solution.py
+++ b/solution.py
@@ -58,13 +58,13 @@
 
 TP_LINE, SUB_RING = 4, 4
 TILE, LAG = 256, 2
-HEADS_AT_ONCE = 4
+HEADS_AT_ONCE = 8
 LOG2E = 1.4426950408889634
 MESH = pl.DeviceIdType.MESH
 
 
 def mix_kernel(
-    lens, queries, new_kv, cache, res, w, out, qv, bv, cv, rows, wv, acc, snd, rin, xin, tot,
+    lens, queries, new_kv, cache, res, w, out, qv, both, bv, cv, rows, wv, acc, snd, rin, xin, tot,
     qsem, wsem, psem, prcv, gsem, grcv, asem, esem, isem, tsem, tend, osem,
 ):
     t, s = lax.axis_index("tp"), lax.axis_index("sub")
@@ -91,11 +91,10 @@
 
     first = [
         pltpu.make_async_copy(src, dst, qsem.at[n])
-        for n, (src, dst) in enumerate(((queries, qv), (new_kv, bv), (cache, cv)))
+        for n, (src, dst) in enumerate(((queries, qv), (new_kv, both), (cache, cv)))
     ]
     for copy in first:
         copy.start()
-    lax.fori_loop(0, tiles, start_load, 0)
 
     barrier = pltpu.get_barrier_semaphore()
     for peer in (sibling, across):
@@ -130,6 +129,9 @@
 
     for copy in first:
         copy.wait()
+    which = lax.broadcasted_iota(jnp.int32, both.shape, 1)
+    for i in range(2):
+        bv[i] = jnp.sum(jnp.where(which == i, both[...].astype(jnp.float32), 0.0), axis=1).astype(bv.dtype)
     capacity = cv.shape[1]
     held = lax.broadcasted_iota(jnp.int32, (1, capacity), 1) < lens[0]
     bias = jnp.where(held, 0.0, -jnp.inf).astype(jnp.float32)
@@ -139,18 +141,21 @@
     factor = HD ** (-0.5) * LOG2E
     last = (((1,), (1,)), ((), ()))
 
+    per_group = tiles // groups
+
     def attend(n, carry):
+        lax.fori_loop(n * per_group, (n + 1) * per_group, start_load, 0)
         wide = qv[:, pl.ds(pl.multiple_of(n * span, span), span)]
         q = jnp.concatenate([wide[:, i * HD : (i + 1) * HD] for i in range(HEADS_AT_ONCE)], axis=0)
         old = lax.dot_general(q, cv[0], last, preferred_element_type=jnp.float32) + bias
-        new = lax.dot_general(q, bv[:, :HD], last, preferred_element_type=jnp.float32)
+        new = lax.dot_general(q, bv[0], last, preferred_element_type=jnp.float32)
         new = jnp.where(causal, new, -jnp.inf)
         top = jnp.maximum(jnp.max(old, axis=1, keepdims=True), jnp.max(new, axis=1, keepdims=True))
         old = jnp.exp2((old - top) * factor)
         new = jnp.exp2((new - top) * factor)
         part = 1.0 / (jnp.sum(old, axis=1, keepdims=True) + jnp.sum(new, axis=1, keepdims=True))
         got = jnp.dot((old * part).astype(jnp.bfloat16), cv[1], preferred_element_type=jnp.float32)
-        got += jnp.dot((new * part).astype(jnp.bfloat16), bv[:, HD:], preferred_element_type=jnp.float32)
+        got += jnp.dot((new * part).astype(jnp.bfloat16), bv[1], preferred_element_type=jnp.float32)
         for i in range(HEADS_AT_ONCE):
             at = pl.ds(pl.multiple_of(n * span + i * HD, HD), HD)
             rows[0, mine, at] = got[i * block : (i + 1) * block].astype(jnp.bfloat16)
@@ -312,7 +317,8 @@
         out_specs=anywhere,
         scratch_shapes=[
             pltpu.VMEM((block, depth), jnp.bfloat16),
-            pltpu.VMEM((block, 2 * HD), jnp.bfloat16),
+            pltpu.VMEM((block, 2, HD), jnp.bfloat16),
+            pltpu.VMEM((2, block, HD), jnp.bfloat16),
             pltpu.VMEM((2,) + cache_kv.shape[3:], jnp.bfloat16),
             pltpu.VMEM((2, 2 * block, depth), jnp.bfloat16),
             pltpu.VMEM((tiles, depth, TILE), jnp.bfloat16),
@@ -340,7 +346,7 @@
     )(
         prefix_len,
         queries.reshape(block, depth),
-        block_kv.reshape(block, 2 * HD),
+        block_kv.reshape(block, 2, HD),
         cache_kv.reshape((2,) + cache_kv.shape[3:]),
         residual,
         out_weight,

time: 77.4 us -> 75.5 us (0.975)
  local copies, waits for them, and re-layouts: 4.51 us -> 3.13 us
    unnamed x2 -> x1, local copies, waits for them, and re-layouts: 4.51 us -> 3.13 us
where the time goes in v3:
time: 75.5 us; the launch traced here: 75.3 us
  Pallas kernels  71.5 us (95%)
  local copies, waits for them, and re-layouts  3.13 us (4%)
    pallas_call x1, Pallas kernels, line_shards(): pl.pallas_call(mix_kernel, out_shape=jax.ShapeDtypeStruct((4 * block, wid...  71.5 us
    unnamed x1, local copies, waits for them, and re-layouts  3.13 us

profile of v3, /device:TPU:0, one launch (start us, length us, event | category | flops | bytes accessed | tf_op | source)
XLA Modules:
  0.0 75.3 jit_solution(297702556150235073)
XLA Ops:
  0.7 71.5 %shard_map.64 = bf16[256,4096]{1,0:T(8,128)(2,1)} custom-call(s32[1]{0:T(128)S(6)} %copy.8.lens, bf16[64,4096]{1,0:T(8,128)(2,1)} %bitcast.3, bf16[64,2,128]{2,1,0:T(2,128)(2,1)} %bitcast.5, bf16[2,1024,128]{2,1,0:T(8,128)(2,1)} %bitcast.4, bf16[64,4096]{1,0:T(8,128)(2,1)} %res.1, bf16[4096,4096]{1,0:T(8,128)(2,1)} %w.1), custom_call_target="tpu_custom_call" | custom-call | tf_op jit(solution)/shard_map/pallas_call | solution.py:306
  72.2 3.1 %copy.9 = bf16[256,4096]{1,0:T(8,128)(2,1)} copy(bf16[256,4096]{1,0:T(8,128)(2,1)} %shard_map.64) | data formatting | bytes 4194304
